TPU v7x, 32 devices: a whole 2x2x4 slice. The times are simulated.
32 devices in a mesh: groups: 2 (over x), seq: 16 (over z, y, core).
Axes of the slice: x: 2, y: 2, z: 4, core: 2. Of those that a mesh axis runs over, the one named last changes fastest.
Arguments:
- tokens: bfloat16 [32768, 1024], P(('groups', 'seq')), parts along dimension 0, may hold values from -6 to 6
- doc_start: int32 [32768], P(('groups', 'seq')), parts along dimension 0, may hold values from 0 to 1
- level_index: int32 [32768], P(('groups', 'seq')), parts along dimension 0, may hold values from 0 to 63
- level_table: float32 [64, 18], replicated, may hold values from 0.0004 to 4.1, as said below
- conv_weight: float32 [4, 1024], replicated, may hold values from -3 to 3
- query_weight: bfloat16 [1024, 1024], replicated, may hold values from -0.1875 to 0.1875
- key_weight: bfloat16 [1024, 1024], replicated, may hold values from -0.1875 to 0.1875
- value_weight: bfloat16 [1024, 1024], replicated, may hold values from -0.1875 to 0.1875
- norm_gain: float32 [1024], replicated, may hold values from 0.5 to 1.5
Outputs:
- mixed: bfloat16 [32768, 1024], P(('groups', 'seq')), parts along dimension 0
There are 2 independent parts, one for each index of `groups`. A program takes and returns all parts, laid end to end along the dimension named above; an argument that names none is the same for every part. Nothing has to cross between parts.
Inputs may be any that keep to these rules, and one draw needn't show every extreme that they name: `level_table`: positive entries.
All inputs are finite; a program needn't handle non-finite values.
Results may differ from a plain program's by a relative error of at most 0.007.
Values may be sent and summed in bfloat16 or wider, within the bound.
A program may use at most 128 MiB of HBM per device.

v0:
```python
import jax
import jax.numpy as jnp
from jax import lax
from jax.sharding import PartitionSpec as P

HEADS = 8
HEAD_DIM = 128


highest = lax.Precision.HIGHEST
epsilon = 1e-05


def from_behind(value, axis, by):
    size = lax.axis_size(axis)
    pairs = [(i, i + by) for i in range(size) if 0 <= i + by < size]
    return lax.ppermute(value, axis, pairs)


def swapped(block, axis, apart):
    count = lax.axis_size(axis)
    route = []
    for low in range(count):
        high = low | 1 << apart
        if high != low and high < count:
            route += [(low, high), (high, low)]
    return lax.ppermute(block, axis, route)


def bit_count(values, bit_width):
    counted = jnp.zeros_like(values)
    for bit_index in range(bit_width):
        counted = counted + (values >= 1 << bit_index).astype(jnp.int32)
    return counted


def shards(
    tokens,
    doc_start,
    level_index,
    level_table,
    conv_weight,
    query_weight,
    key_weight,
    value_weight,
    norm_gain,
):
    row_count = tokens.shape[0]
    tap_count = conv_weight.shape[0]
    local_bits = row_count.bit_length() - 1
    local_doc = jnp.cumsum(doc_start)
    last_doc = local_doc[row_count - 1]
    rim_keep = (local_doc[row_count - tap_count + 1 :] == last_doc).astype(tokens.dtype)
    rim_rows = tokens[row_count - tap_count + 1 :] * rim_keep[:, None]
    carried = from_behind(rim_rows, "seq", 1)
    extended = jnp.concatenate([carried, tokens], 0)
    ext_doc = jnp.concatenate([jnp.zeros((tap_count - 1,), jnp.int32), local_doc], 0)
    conv_sum = jnp.zeros(tokens.shape, jnp.float32)
    for tap_index in range(tap_count):
        low_row = tap_count - 1 - tap_index
        same_doc = (ext_doc[low_row : low_row + row_count] == local_doc).astype(jnp.float32)
        conv_sum = (
            conv_sum
            + conv_weight[tap_index][None, :]
            * extended[low_row : low_row + row_count]
            * same_doc[:, None]
        )
    conv_out = conv_sum.astype(jnp.bfloat16)
    queries = (
        jnp.dot(conv_out, query_weight, preferred_element_type=jnp.float32)
        .astype(jnp.bfloat16)
        .reshape(row_count, HEADS, HEAD_DIM)
    )
    key_rows = (
        jnp.dot(conv_out, key_weight, preferred_element_type=jnp.float32)
        .astype(jnp.bfloat16)
        .reshape(row_count, HEADS, HEAD_DIM)
    )
    values = (
        jnp.dot(conv_out, value_weight, preferred_element_type=jnp.float32)
        .astype(jnp.bfloat16)
        .reshape(row_count, HEADS, HEAD_DIM)
    )
    onehot = (
        level_index[:, None] == jnp.arange(level_table.shape[0], dtype=jnp.int32)[None, :]
    ).astype(jnp.float32)
    level_weight = jnp.dot(
        onehot, level_table, precision=highest, preferred_element_type=jnp.float32
    )
    tail_mask = (local_doc == last_doc).astype(jnp.bfloat16)
    key_tail = key_rows * tail_mask[:, None, None]
    own_state = jnp.einsum("nhd,nhe->hde", key_tail, values, preferred_element_type=jnp.float32)
    own_open = (last_doc == 0).astype(jnp.float32)
    my_index = lax.axis_index("seq")
    chain_steps = lax.axis_size("seq").bit_length() - 1
    agg_state = own_state
    agg_open = own_open
    before_open = jnp.float32(1.0)
    level_states = []
    for bit_index in range(chain_steps):
        if bit_index < chain_steps - 1:
            other_state, other_open = swapped((agg_state, agg_open), "seq", bit_index)
        else:
            other_state, other_open = from_behind((agg_state, agg_open), "seq", 1 << bit_index)
        is_right = my_index // (1 << bit_index) % 2 == 1
        level_states.append(jnp.where(is_right, before_open, 0.0) * other_state)
        if bit_index < chain_steps - 1:
            left_state = jnp.where(is_right, other_state, agg_state)
            right_state = jnp.where(is_right, agg_state, other_state)
            left_open = jnp.where(is_right, other_open, agg_open)
            right_open = jnp.where(is_right, agg_open, other_open)
            before_open = before_open * jnp.where(is_right, other_open, 1.0)
            agg_state = right_state + right_open * left_state
            agg_open = left_open * right_open
    block_rows = min(512, row_count)
    key_pos = jnp.arange(row_count, dtype=jnp.int32)
    results = []
    for first_row in range(0, row_count, block_rows):
        query_pos = jnp.arange(first_row, first_row + block_rows, dtype=jnp.int32)
        level_of = bit_count(jnp.bitwise_xor(query_pos[:, None], key_pos[None, :]), local_bits)
        same_doc = (local_doc[first_row : first_row + block_rows, None] == local_doc[None, :]) & (
            query_pos[:, None] >= key_pos[None, :]
        )
        weight_rows = level_weight[first_row : first_row + block_rows]
        weight = jnp.zeros((block_rows, row_count), jnp.float32)
        for level_id in range(local_bits + 1):
            weight = weight + jnp.where(
                level_of == level_id, weight_rows[:, level_id : level_id + 1], 0.0
            )
        weight = jnp.where(same_doc, weight, 0.0)
        scores = jnp.einsum(
            "thd,shd->hts",
            queries[first_row : first_row + block_rows],
            key_rows,
            preferred_element_type=jnp.float32,
        )
        weighted = (scores * weight[None]).astype(jnp.bfloat16)
        results.append(
            jnp.einsum("hts,shd->thd", weighted, values, preferred_element_type=jnp.float32)
        )
    near_sum = jnp.concatenate(results, 0)
    token_gate = (local_doc == 0).astype(jnp.float32)
    query_wide = queries.astype(jnp.float32)
    combined = near_sum
    for bit_index, level_state in enumerate(level_states):
        product = jnp.einsum("thd,hde->the", query_wide, level_state, precision=highest)
        scale_now = level_weight[:, local_bits + 1 + bit_index] * token_gate
        combined = combined + scale_now[:, None, None] * product
    inv_norm = lax.rsqrt(jnp.mean(combined * combined, axis=-1, keepdims=True) + epsilon)
    gain_heads = norm_gain.reshape(HEADS, HEAD_DIM)
    return (
        (combined * inv_norm * gain_heads[None])
        .reshape(row_count, HEADS * HEAD_DIM)
        .astype(jnp.bfloat16)
    )


def solution(mesh):
    in_specs = (
        P(("groups", "seq"), None),
        P(("groups", "seq")),
        P(("groups", "seq")),
        P(),
        P(),
        P(),
        P(),
        P(),
        P(),
    )
    out_specs = P(("groups", "seq"), None)
    return jax.shard_map(shards, mesh=mesh, in_specs=in_specs, out_specs=out_specs, check_vma=False)
```

profile of v0, /device:TPU:28, one launch (start us, length us, event | category | flops | bytes accessed | tf_op | source)
XLA Modules:
  0.0 118.9 jit_solution(13723291301358879340)
XLA Ops:
  0.0 1.1 reduce-window.9
  1.1 0.1 slice.171
  1.2 0.1 slice_reduce_fusion
  1.3 1.2 fusion.41
  2.6 0.1 broadcast_select_fusion.3
  2.6 0.6 slice.174
  3.9 1.0 collective-permute-start.2
  4.9 0.7 compare_convert_fusion.1
  5.6 0.8 slice_multiply_fusion
  6.4 2.4 %collective-permute-start = (bf16[3,1024]{1,0:T(4,128)(2,1)S(1)}, bf16[3,1024]{1,0:T(4,128)(2,1)S(1)}, u32[]{:S(2)}, u32[]{:S(2)}) collective-permute-start(bf16[3,1024]{1,0:T(4,128)(2,1)S(1)} %slice_multiply_fusion), channel_id=1, source_target_pairs={{0,1},{1,2},{2,3},{3,4},{4,5},{5,6},{6,7},{7,8},{8,9},{9,10},{10,1... | collective-permute-start | bytes 18440 | tf_op jit(solution)/shard_map/ppermute | solution.py:17
  8.9 0.1 fusion.52
  9.0 0.9 fusion.57
  9.9 5.6 %add_select_fusion.1 = f32[512,1024]{1,0:T(8,128)} fusion(f32[512]{0:T(512)S(1)} %bitcast.109, f32[512]{0:T(512)S(1)} %bitcast.110, f32[512]{0:T(512)S(1)} %bitcast.111, f32[512]{0:T(512)S(1)} %bitcast.112, f32[512]{0:T(512)S(1)} %bitcast.113, f32[512]{0:T(512)S(1)} %bitcast.114, f32[512]{0:T(512)S(1)} %bitcast.115, f32[512]{0:T(512)S(1)} %bitcast.117, ...), kind=kLoop, calls=%fused_computation.32 | loop fusion | flops 34603008 | bytes 2125824 | tf_op jit(solution)/shard_map/jit(_where)/select_n | solution.py:130
  15.5 5.7 %add_select_fusion = f32[512,1024]{1,0:T(8,128)} fusion(f32[512]{0:T(512)S(1)} %bitcast.97, f32[512]{0:T(512)S(1)} %bitcast.98, f32[512]{0:T(512)S(1)} %bitcast.99, f32[512]{0:T(512)S(1)} %bitcast.100, f32[512]{0:T(512)S(1)} %bitcast.101, f32[512]{0:T(512)S(1)} %bitcast.102, f32[512]{0:T(512)S(1)} %bitcast.103, f32[512]{0:T(512)S(1)} %bitcast.104, ...), kind=kLoop, calls=%fused_computation.18 | loop fusion | flops 34603008 | bytes 2127872 | tf_op jit(solution)/shard_map/jit(_where)/select_n | solution.py:130
  21.2 0.6 compare_convert_fusion
  23.2 1.9 %collective-permute-start.4 = (f32[]{:T(128)}, f32[]{:T(128)}, u32[]{:S(2)}, u32[]{:S(2)}) collective-permute-start(f32[]{:T(128)} %mul.269), channel_id=1, source_target_pairs={{0,2},{2,0},{1,3},{3,1},{4,6},{6,4},{5,7},{7,5},{8,10},{10,8},{9,1... | collective-permute-start | bytes 20 | tf_op jit(solution)/shard_map/ppermute | solution.py:27
  25.7 1.2 %collective-permute-done.4 = f32[]{:T(128)} collective-permute-done((f32[]{:T(128)}, f32[]{:T(128)}, u32[]{:S(2)}, u32[]{:S(2)}) %collective-permute-start.4) | collective-permute-done | bytes 36 | tf_op jit(solution)/shard_map/ppermute | solution.py:27
  28.8 1.8 %collective-permute-start.6 = (f32[]{:T(128)}, f32[]{:T(128)}, u32[]{:S(2)}, u32[]{:S(2)}) collective-permute-start(f32[]{:T(128)} %mul.279), channel_id=1, source_target_pairs={{0,4},{4,0},{1,5},{5,1},{2,6},{6,2},{3,7},{7,3},{8,12},{12,8},{9,1... | collective-permute-start | bytes 20 | tf_op jit(solution)/shard_map/ppermute | solution.py:27
  30.6 1.9 %collective-permute-done.6 = f32[]{:T(128)} collective-permute-done((f32[]{:T(128)}, f32[]{:T(128)}, u32[]{:S(2)}, u32[]{:S(2)}) %collective-permute-start.6) | collective-permute-done | bytes 36 | tf_op jit(solution)/shard_map/ppermute | solution.py:27
  33.8 7.6 %add_convert_fusion = bf16[1024,1024]{1,0:T(8,128)(2,1)S(1)} fusion(bf16[1024,1024]{1,0:T(8,128)(2,1)} %param.9, bf16[3,1024]{1,0:T(4,128)(2,1)S(1)} %collective-permute-done, f32[1024]{0:T(1024)S(1)} %get-tuple-element.43, f32[1024]{0:T(1024)S(1)} %bitcast.91, f32[1024]{0:T(1024)S(1)} %get-tuple-element.44, f32[1024]{0:T(1024)S(1)} %bitcast.92, ...), kind=kLoop, calls=%fused_computation.8 | loop fusion | flops 25165824 | bytes 4229120 | tf_op jit(solution)/shard_map/convert_element_type | solution.py:68
  41.4 0.0 copy-start.8
  41.4 2.4 %convolution_convert_fusion = bf16[1024,1024]{0,1:T(8,128)(2,1)S(1)} fusion(bf16[1024,1024]{1,0:T(8,128)(2,1)S(1)} %add_convert_fusion, bf16[1024,1024]{1,0:T(8,128)(2,1)S(1)} %copy-done), kind=kOutput, calls=%fused_computation.48 | convolution fusion | flops 2148532224 | bytes 6291456 | tf_op jit(solution)/shard_map/dot_general | solution.py:75
  43.8 2.4 %convolution_convert_fusion.2 = bf16[1024,1024]{0,1:T(8,128)(2,1)S(1)} fusion(bf16[1024,1024]{1,0:T(8,128)(2,1)S(1)} %add_convert_fusion, bf16[1024,1024]{1,0:T(8,128)(2,1)S(1)} %copy-done.8), kind=kOutput, calls=%fused_computation.50 | convolution fusion | flops 2148532224 | bytes 6291456 | tf_op jit(solution)/shard_map/dot_general | solution.py:80
  46.2 0.0 copy-start.9
  46.2 0.7 fusion.7
  47.0 0.6 copy-done.11
  47.6 1.0 copy-done.9
  48.6 2.4 %convolution_convert_fusion.1 = bf16[1024,1024]{0,1:T(8,128)(2,1)S(1)} fusion(bf16[1024,1024]{1,0:T(8,128)(2,1)S(1)} %add_convert_fusion, bf16[1024,1024]{1,0:T(8,128)(2,1)S(1)} %copy-done.9), kind=kOutput, calls=%fused_computation.49 | convolution fusion | flops 2148532224 | bytes 6291456 | tf_op jit(solution)/shard_map/dot_general | solution.py:70
  51.0 0.0 copy-start.1
  51.0 1.6 %fusion.53 = (bf16[512,1024]{0,1:T(8,128)(2,1)}, bf16[512,1024]{0,1:T(8,128)(2,1)}) fusion(bf16[1024,1024]{0,1:T(8,128)(2,1)S(1)} %convolution_convert_fusion.1), kind=kLoop, calls=%fused_computation.94 | loop fusion | bytes 4194304 | tf_op jit(solution)/shard_map/slice | solution.py:133
  52.6 0.4 copy-done.1
  53.0 0.8 copy-done.5
  53.8 0.1 multiply_add_fusion.2
  53.9 0.6 collective-permute-start.3
  54.4 9.6 %fusion.32 = f32[512,8,128]{0,2,1:T(8,128)} fusion(bf16[1024,8,128]{0,2,1:T(8,128)(2,1)} %bitcast.125, bf16[512,8,128]{0,2,1:T(8,128)(2,1)} %bitcast.83, bf16[1024,8,128]{0,2,1:T(8,128)(2,1)} %bitcast.122, f32[512,1024]{1,0:T(8,128)} %add_select_fusion.1), kind=kOutput, calls=%fused_computation.52 | convolution fusion | flops 2155872256 | bytes 9437184 | tf_op jit(solution)/shard_map/hts,shd->thd/dot_general | solution.py:139
  64.0 3.4 %collective-permute-done.3 = f32[8,128,128]{2,1,0:T(8,128)} collective-permute-done((f32[8,128,128]{2,1,0:T(8,128)S(1)}, f32[8,128,128]{2,1,0:T(8,128)}, u32[]{:S(2)}, u32[]{:S(2)}) %collective-permute-start.3) | collective-permute-done | bytes 524320 | tf_op jit(solution)/shard_map/ppermute | solution.py:27
  67.4 1.1 multiply_add_fusion.1
  68.5 0.5 collective-permute-start.5
  69.0 9.6 %fusion.31 = f32[512,8,128]{0,2,1:T(8,128)} fusion(bf16[1024,8,128]{0,2,1:T(8,128)(2,1)} %bitcast.126, bf16[512,8,128]{0,2,1:T(8,128)(2,1)} %bitcast.82, bf16[1024,8,128]{0,2,1:T(8,128)(2,1)} %bitcast.123, f32[512,1024]{1,0:T(8,128)} %add_select_fusion), kind=kOutput, calls=%fused_computation.51 | convolution fusion | flops 2155872256 | bytes 9437184 | tf_op jit(solution)/shard_map/hts,shd->thd/dot_general | solution.py:139
  78.6 3.6 %fusion.39 = f32[8,128,1024]{2,1,0:T(8,128)S(1)} fusion(bf16[1024,8,128]{0,2,1:T(8,128)(2,1)} %bitcast.77, f32[8,128,128]{2,1,0:T(8,128)S(1)} %copy-done.6, f32[]{:T(128)S(6)} %select_n.295), kind=kOutput, calls=%fused_computation.62 | convolution fusion | flops 1610743808 | bytes 6815748 | tf_op jit(solution)/shard_map/thd,hde->the/dot_general | solution.py:146
  82.2 1.1 multiply_add_fusion
  83.4 1.6 %collective-permute-start.7 = (f32[8,128,128]{2,1,0:T(8,128)S(1)}, f32[8,128,128]{2,1,0:T(8,128)S(1)}, u32[]{:S(2)}, u32[]{:S(2)}) collective-permute-start(f32[8,128,128]{2,1,0:T(8,128)S(1)} %multiply_add_fusion), channel_id=1, source_target_pairs={{0,8},{1,9},{2,10},{3,11},{4,12},{5,13},{6,14},{7,15},{16,24},{17,... | collective-permute-start | bytes 1572872 | tf_op jit(solution)/shard_map/ppermute | solution.py:17
  84.9 3.0 %fusion.37 = f32[8,128,1024]{2,1,0:T(8,128)S(1)} fusion(bf16[1024,8,128]{0,2,1:T(8,128)(2,1)S(1)} %bitcast.78, f32[8,128,128]{2,1,0:T(8,128)} %collective-permute-done.3, f32[]{:T(128)S(6)} %select_n.299), kind=kOutput, calls=%fused_computation.59 | convolution fusion | flops 1610743808 | bytes 6815748 | tf_op jit(solution)/shard_map/thd,hde->the/dot_general | solution.py:146
  87.9 3.1 %fusion.35 = f32[8,128,1024]{2,1,0:T(8,128)S(1)} fusion(bf16[1024,8,128]{0,2,1:T(8,128)(2,1)S(1)} %bitcast.79, f32[8,128,128]{2,1,0:T(8,128)} %collective-permute-done.5, f32[]{:T(128)S(6)} %select_n.308), kind=kOutput, calls=%fused_computation.56 | convolution fusion | flops 1610743808 | bytes 6815748 | tf_op jit(solution)/shard_map/thd,hde->the/dot_general | solution.py:146
  91.0 18.5 %collective-permute-done.7 = f32[8,128,128]{2,1,0:T(8,128)S(1)} collective-permute-done((f32[8,128,128]{2,1,0:T(8,128)S(1)}, f32[8,128,128]{2,1,0:T(8,128)S(1)}, u32[]{:S(2)}, u32[]{:S(2)}) %collective-permute-start.7) | collective-permute-done | bytes 524320 | tf_op jit(solution)/shard_map/ppermute | solution.py:17
  109.5 3.5 %multiply_reduce_fusion = (f32[1024,8]{0,1:T(8,128)S(1)}, f32[1024,8,128]{0,2,1:T(8,128)S(1)}) fusion(bf16[1024,8,128]{0,2,1:T(8,128)(2,1)S(1)} %bitcast.80, f32[8,128,128]{2,1,0:T(8,128)S(1)} %collective-permute-done.7, f32[]{:T(128)S(6)} %select_n.317, f32[1024]{0:T(1024)S(1)} %get-tuple-element.47, f32[8,128,1024]{2,1,0:T(8,128)S(1)} %fusion.35, ...), kind=kOutput, calls=%fused_computation.7 | convolution fusion | flops 1622269952 | bytes 23642116 | tf_op jit(solution)/shard_map/thd,hde->the/dot_general | solution.py:146
  113.1 1.9 %multiply_convert_fusion.2 = bf16[1024,8,128]{0,2,1:T(8,128)(2,1)} fusion(f32[1024,8,128]{0,2,1:T(8,128)S(1)} %get-tuple-element.49, f32[8,128]{1,0:T(8,128)S(1)} %bitcast.120, f32[1024,8]{0,1:T(8,128)S(1)} %add_rsqrt_fusion), kind=kLoop, calls=%fused_computation.6 | loop fusion | flops 3145728 | bytes 6328320 | tf_op jit(solution)/shard_map/convert_element_type | solution.py:154
  114.9 3.9 %copy.29 = bf16[1024,1024]{1,0:T(8,128)(2,1)} copy(bf16[1024,1024]{0,1:T(8,128)(2,1)} %bitcast.81) | data formatting | bytes 4194304 | tf_op jit(solution)/shard_map/convert_element_type | solution.py:154
  (30 shorter events, 0.2 us)
Async XLA Ops:
  0.0 41.4 %copy-start = (bf16[1024,1024]{1,0:T(8,128)(2,1)S(1)}, bf16[1024,1024]{1,0:T(8,128)(2,1)}, u32[]{:S(2)}) copy-start(bf16[1024,1024]{1,0:T(8,128)(2,1)} %param.15) | copy-start | bytes 6291460
  3.9 18.0 %collective-permute-start.2 = (f32[]{:T(128)}, f32[]{:T(128)}, u32[]{:S(2)}, u32[]{:S(2)}) collective-permute-start(f32[]{:T(128)} %convert_element_type.636), channel_id=1, source_target_pairs={{0,1},{1,0},{2,3},{3,2},{4,5},{5,4},{6,7},{7,6},{8,9},{9,8},{10,11... | collective-permute-start | bytes 20 | tf_op jit(solution)/shard_map/ppermute | solution.py:27
  6.4 27.4 %collective-permute-start = (bf16[3,1024]{1,0:T(4,128)(2,1)S(1)}, bf16[3,1024]{1,0:T(4,128)(2,1)S(1)}, u32[]{:S(2)}, u32[]{:S(2)}) collective-permute-start(bf16[3,1024]{1,0:T(4,128)(2,1)S(1)} %slice_multiply_fusion), channel_id=1, source_target_pairs={{0,1},{1,2},{2,3},{3,4},{4,5},{5,6},{6,7},{7,8},{8,9},{9,10},{10,1... | collective-permute-start | bytes 18440 | tf_op jit(solution)/shard_map/ppermute | solution.py:17
  23.2 3.7 %collective-permute-start.4 = (f32[]{:T(128)}, f32[]{:T(128)}, u32[]{:S(2)}, u32[]{:S(2)}) collective-permute-start(f32[]{:T(128)} %mul.269), channel_id=1, source_target_pairs={{0,2},{2,0},{1,3},{3,1},{4,6},{6,4},{5,7},{7,5},{8,10},{10,8},{9,1... | collective-permute-start | bytes 20 | tf_op jit(solution)/shard_map/ppermute | solution.py:27
  28.8 3.7 %collective-permute-start.6 = (f32[]{:T(128)}, f32[]{:T(128)}, u32[]{:S(2)}, u32[]{:S(2)}) collective-permute-start(f32[]{:T(128)} %mul.279), channel_id=1, source_target_pairs={{0,4},{4,0},{1,5},{5,1},{2,6},{6,2},{3,7},{7,3},{8,12},{12,8},{9,1... | collective-permute-start | bytes 20 | tf_op jit(solution)/shard_map/ppermute | solution.py:27
  41.4 2.4 %copy-start.8 = (bf16[1024,1024]{1,0:T(8,128)(2,1)S(1)}, bf16[1024,1024]{1,0:T(8,128)(2,1)}, u32[]{:S(2)}) copy-start(bf16[1024,1024]{1,0:T(8,128)(2,1)} %param.16) | copy-start | bytes 6291460
  43.8 2.4 %copy-start.10 = (bf16[1024,1024]{0,1:T(8,128)(2,1)}, bf16[1024,1024]{0,1:T(8,128)(2,1)S(1)}, u32[]{:S(2)}) copy-start(bf16[1024,1024]{0,1:T(8,128)(2,1)S(1)} %convolution_convert_fusion) | copy-start | bytes 6291460
  46.2 1.4 %copy-start.11 = (bf16[1024,1024]{0,1:T(8,128)(2,1)}, bf16[1024,1024]{0,1:T(8,128)(2,1)S(1)}, u32[]{:S(2)}) copy-start(bf16[1024,1024]{0,1:T(8,128)(2,1)S(1)} %convolution_convert_fusion.2) | copy-start | bytes 6291460
  46.2 2.3 %copy-start.9 = (bf16[1024,1024]{1,0:T(8,128)(2,1)S(1)}, bf16[1024,1024]{1,0:T(8,128)(2,1)}, u32[]{:S(2)}) copy-start(bf16[1024,1024]{1,0:T(8,128)(2,1)} %param.14) | copy-start | bytes 6291460
  47.6 5.4 %collective-permute-start.1 = (f32[8,128,128]{2,1,0:T(8,128)S(1)}, f32[8,128,128]{2,1,0:T(8,128)S(1)}, u32[]{:S(2)}, u32[]{:S(2)}) collective-permute-start(f32[8,128,128]{2,1,0:T(8,128)S(1)} %fusion.7), channel_id=1, source_target_pairs={{0,1},{1,0},{2,3},{3,2},{4,5},{5,4},{6,7},{7,6},{8,9},{9,8},{10,11... | collective-permute-start | bytes 1572872 | tf_op jit(solution)/shard_map/ppermute | solution.py:27
  51.0 2.0 %copy-start.1 = (bf16[1024,1024]{0,1:T(8,128)(2,1)}, bf16[1024,1024]{0,1:T(8,128)(2,1)S(1)}, u32[]{:S(2)}) copy-start(bf16[1024,1024]{0,1:T(8,128)(2,1)S(1)} %convolution_convert_fusion.1) | copy-start | bytes 6291460
  53.0 0.8 copy-start.5
  53.9 13.5 %collective-permute-start.3 = (f32[8,128,128]{2,1,0:T(8,128)S(1)}, f32[8,128,128]{2,1,0:T(8,128)}, u32[]{:S(2)}, u32[]{:S(2)}) collective-permute-start(f32[8,128,128]{2,1,0:T(8,128)S(1)} %multiply_add_fusion.2), channel_id=1, source_target_pairs={{0,2},{2,0},{1,3},{3,1},{4,6},{6,4},{5,7},{7,5},{8,10},{10,8},{9,1... | collective-permute-start | bytes 1572872 | tf_op jit(solution)/shard_map/ppermute | solution.py:27
  68.5 13.7 %collective-permute-start.5 = (f32[8,128,128]{2,1,0:T(8,128)S(1)}, f32[8,128,128]{2,1,0:T(8,128)}, u32[]{:S(2)}, u32[]{:S(2)}) collective-permute-start(f32[8,128,128]{2,1,0:T(8,128)S(1)} %multiply_add_fusion.1), channel_id=1, source_target_pairs={{0,4},{4,0},{1,5},{5,1},{2,6},{6,2},{3,7},{7,3},{8,12},{12,8},{9,1... | collective-permute-start | bytes 1572872 | tf_op jit(solution)/shard_map/ppermute | solution.py:27
  69.0 9.6 %copy-start.6 = (f32[8,128,128]{2,1,0:T(8,128)S(1)}, f32[8,128,128]{2,1,0:T(8,128)}, u32[]{:S(2)}) copy-start(f32[8,128,128]{2,1,0:T(8,128)} %copy-done.5) | copy-start | bytes 1572868
  78.6 6.3 %copy-start.2 = (bf16[1024,1024]{0,1:T(8,128)(2,1)S(1)}, bf16[1024,1024]{0,1:T(8,128)(2,1)}, u32[]{:S(2)}) copy-start(bf16[1024,1024]{0,1:T(8,128)(2,1)} %copy-done.1) | copy-start | bytes 6291460
  83.4 26.2 %collective-permute-start.7 = (f32[8,128,128]{2,1,0:T(8,128)S(1)}, f32[8,128,128]{2,1,0:T(8,128)S(1)}, u32[]{:S(2)}, u32[]{:S(2)}) collective-permute-start(f32[8,128,128]{2,1,0:T(8,128)S(1)} %multiply_add_fusion), channel_id=1, source_target_pairs={{0,8},{1,9},{2,10},{3,11},{4,12},{5,13},{6,14},{7,15},{16,24},{17,... | collective-permute-start | bytes 1572872 | tf_op jit(solution)/shard_map/ppermute | solution.py:17
  87.9 21.6 %copy-start.3 = (f32[512,8,128]{0,2,1:T(8,128)S(1)}, f32[512,8,128]{0,2,1:T(8,128)}, u32[]{:S(2)}) copy-start(f32[512,8,128]{0,2,1:T(8,128)} %fusion.32) | copy-start | bytes 6291460
  87.9 21.6 %copy-start.4 = (f32[512,8,128]{0,2,1:T(8,128)S(1)}, f32[512,8,128]{0,2,1:T(8,128)}, u32[]{:S(2)}) copy-start(f32[512,8,128]{0,2,1:T(8,128)} %fusion.31) | copy-start | bytes 6291460
  109.5 3.5 %copy-start.7 = (f32[1024]{0:T(1024)S(1)}, f32[1024]{0:T(1024)}, u32[]{:S(2)}) copy-start(f32[1024]{0:T(1024)} %param.17) | copy-start | bytes 12292
where the time goes:
time: 120 us; the launch traced here: 119 us
  matrix products  41.4 us (34%)
  other arithmetic  26.6 us (22%)
  waiting for transfers between devices  25 us (21%)
  local copies, waits for them, and re-layouts  10.1 us (8%)
  starting transfers between devices  9.75 us (8%)
  between operations  6.1 us (5%)
    dot_general x2, matrix products, shards(): jnp.einsum('hts,shd->thd', weighted, values, preferred_element_type=jnp.f...  19.1 us
    ppermute x2, waiting for transfers between devices, from_behind(): return lax.ppermute(value, axis, pairs)  18.5 us
    dot_general x4, matrix products, shards(): jnp.einsum('thd,hde->the', query_wide, level_state, precision=highest)  13.2 us
    select_n x2, other arithmetic, shards(): weight = jnp.where(same_doc, weight, 0.0)  11.3 us
    convert_element_type x1, other arithmetic, shards(): conv_out = conv_sum.astype(jnp.bfloat16)  7.63 us
    ppermute x6, waiting for transfers between devices, swapped(): return lax.ppermute(block, axis, route)  6.47 us
    ppermute x6, starting transfers between devices, swapped(): return lax.ppermute(block, axis, route)  5.8 us
    ppermute x2, starting transfers between devices, from_behind(): return lax.ppermute(value, axis, pairs)  3.95 us
  transfers between devices with their start and end apart: 8, of which 4 were waited for; matrix products, arithmetic and copies ran while one was open for 40% of the time, Pallas kernels for 0%

commit v1 on v0

v1 whole, which is shorter than its diff:
```python
import functools

import jax
import jax.numpy as jnp
from jax import lax
from jax.experimental import pallas as pl
from jax.experimental.pallas import tpu as pltpu
from jax.sharding import PartitionSpec as P

HEADS = 8
HEAD_DIM = 128
LANES = 128
EDGE = 16

highest = lax.Precision.HIGHEST
epsilon = 1e-05
f32 = jnp.float32
bf16 = jnp.bfloat16


def dot(a, b, contract=((1,), (0,)), precision=None):
    return lax.dot_general(a, b, (contract, ((), ())), precision=precision, preferred_element_type=f32)


def layer(
    count,
    ds_ref, li_ref, table_ref, taps_ref, gain_ref, tok_ref, wq_hbm, wk_hbm, wv_hbm,
    out_ref,
    wq, wk, wv, turn, docs, dext, tail, lam, lamfar, weight, ext, conv, q, k, v, near,
    state, agg, flag_agg, flag_before, coef, send, recv, rim, halo,
    w_sem, send_sem, recv_sem, fwd_send, fwd_recv, rim_sem,
):
    rows, width = tok_ref.shape
    tiles = rows // LANES
    taps = taps_ref.shape[0]
    bits = count.bit_length() - 1
    local_bits = rows.bit_length() - 1
    tile_bits = LANES.bit_length() - 1
    half_heads = HEADS // 2
    half = half_heads * HEAD_DIM
    me = lax.axis_index("seq")
    core = lax.rem(me, 2)
    sibling = me + 1 - 2 * core

    def side(bit):
        return lax.rem(me // (1 << bit), 2)

    def partner(bit):
        return me + (1 - 2 * side(bit)) * (1 << bit)

    ahead, behind = lax.rem(me + 1, count), lax.rem(me + count - 1, count)
    barrier = pltpu.get_barrier_semaphore()
    greeted = [ahead, behind] + [partner(bit) for bit in range(bits)]
    for other in greeted:
        pl.semaphore_signal(barrier, inc=1, device_id={"seq": other}, device_id_type=pl.DeviceIdType.MESH)

    loads = [
        pltpu.make_async_copy(src, dst, w_sem.at[i])
        for i, (src, dst) in enumerate(((wk_hbm, wk), (wv_hbm, wv), (wq_hbm, wq)))
    ]
    for load in loads:
        load.start()

    def remote(src, dst, s_sem, r_sem, to):
        return pltpu.make_async_remote_copy(
            src_ref=src, dst_ref=dst, send_sem=s_sem, recv_sem=r_sem,
            device_id={"seq": to}, device_id_type=pl.DeviceIdType.MESH,
        )

    sub = lax.broadcasted_iota(jnp.int32, (LANES, LANES), 0)
    lane = lax.broadcasted_iota(jnp.int32, (LANES, LANES), 1)
    upper = (sub <= lane).astype(f32).astype(bf16)
    counted = dot(ds_ref[...].astype(f32).astype(bf16), upper)
    running = jnp.zeros((1, 1), f32)
    turn[...] = jnp.zeros_like(turn)
    for i in range(tiles):
        turn[i : i + 1, :] = counted[i : i + 1, :] + running
        docs[i : i + 1, :] = counted[i : i + 1, :] + running
        running = running + counted[i : i + 1, LANES - 1 : LANES]
    turn[tiles : 2 * tiles, :] = li_ref[...].astype(f32)
    turned = jnp.transpose(turn[...])
    last_doc = running
    dext[0:8, :] = jnp.zeros((8, LANES), f32)
    for i in range(tiles):
        column = jnp.broadcast_to(turned[:, i : i + 1], (LANES, LANES))
        dext[8 + i * LANES : 8 + (i + 1) * LANES, :] = column
        tail[i * LANES : (i + 1) * LANES, :] = (column == last_doc).astype(f32).astype(bf16)
    own_open = jnp.broadcast_to((last_doc == 0.0).astype(f32), (8, LANES))
    flag_agg[...] = own_open
    flag_before[...] = jnp.ones((8, LANES), f32)

    for j in range(width // LANES):
        cols = slice(j * LANES, (j + 1) * LANES)
        rim[:, cols] = tok_ref[rows - EDGE : rows, cols] * tail[rows - EDGE : rows, :]
    pl.semaphore_wait(barrier, len(greeted))
    rim_copy = remote(rim, halo, rim_sem.at[0], rim_sem.at[1], ahead)

    @pl.when(me < count - 1)
    def _():
        rim_copy.start()

    chunk = 64

    def conv_chunk(first):
        ext[pl.ds(8 + first, chunk), :] = tok_ref[pl.ds(first, chunk), :].astype(f32)
        window = pl.ds(first, chunk + 8)
        docs_here = dext[window, :]
        same = [(pltpu.roll(docs_here, t, 0) == docs_here).astype(f32)[8:] for t in range(1, taps)]
        for j in range(width // LANES):
            cols = slice(j * LANES, (j + 1) * LANES)
            values = ext[window, cols]
            total = taps_ref[0:1, cols] * values[8:]
            for t in range(1, taps):
                total = total + taps_ref[t : t + 1, cols] * pltpu.roll(values, t, 0)[8:] * same[t - 1]
            conv[pl.ds(first, chunk), cols] = total.astype(bf16)

    ext[8 : 8 + chunk, :] = tok_ref[0:chunk, :].astype(f32)

    @pl.loop(1, rows // chunk)
    def _(i):
        conv_chunk(pl.multiple_of(i * chunk, chunk))

    @pl.when(me > 0)
    def _():
        rim_copy.wait_recv()

    @pl.when(me == 0)
    def _():
        halo[...] = jnp.zeros_like(halo)

    ext[0:8, :] = halo[...].astype(f32)[EDGE - 8 : EDGE, :]
    conv_chunk(0)

    def project(w, out, i):
        cols = pl.ds(pl.multiple_of(i * 2 * HEAD_DIM, 2 * HEAD_DIM), 2 * HEAD_DIM)
        made = dot(conv[...], w[:, cols]).astype(bf16)
        out[2 * i] = made[:, :HEAD_DIM]
        out[2 * i + 1] = made[:, HEAD_DIM:]

    loads[0].wait()
    loads[1].wait()

    @pl.loop(0, HEADS // 2)
    def _(i):
        project(wk, k, i)
        project(wv, v, i)
        for s in range(2):
            h = 2 * i + s
            made = dot(k[h] * tail[...], v[h], ((0,), (0,)))
            at = pl.ds(pl.multiple_of(lax.rem(h, half_heads) * HEAD_DIM, HEAD_DIM), HEAD_DIM)
            state[h // half_heads, at, :] = made
            send[0, h // half_heads, at, :] = made.astype(bf16)

    flag_rows = jnp.concatenate([own_open, own_open], 0).astype(bf16)
    for s in range(2):
        send[0, s, half : half + EDGE, :] = flag_rows
    first = remote(send.at[0], recv.at[0], send_sem.at[0], recv_sem.at[0], sibling)
    first.start()

    def step(bit):
        return remote(send.at[bit, core], recv.at[bit, core], send_sem.at[bit], recv_sem.at[bit], partner(bit))

    def forward(bit):
        return remote(recv.at[bit, core], recv.at[bit, core], fwd_send.at[bit], fwd_recv.at[bit], sibling)

    def note_flags(bit):
        other = recv[bit, core, half : half + EDGE, :].astype(f32)[0:8]
        right = side(bit).astype(f32)
        before = flag_before[...]
        coef[bit] = right * before
        flag_before[...] = before * ((1.0 - right) + right * other)
        return other, right

    def absorb(bit):
        other, right = note_flags(bit)
        mine = flag_agg[...]
        of_agg = (right + (1.0 - right) * other)[0:1]
        of_other = ((1.0 - right) + right * mine)[0:1]
        source = state.at[core] if bit == 0 else agg
        total = of_agg * source[...] + of_other * recv[bit, core, 0:half, :].astype(f32)
        agg[...] = total
        send[bit + 1, core, 0:half, :] = total.astype(bf16)
        joined = mine * other
        flag_agg[...] = joined
        send[bit + 1, core, half : half + EDGE, :] = jnp.concatenate([joined, joined], 0).astype(bf16)
        step(bit + 1).start()

    loads[2].wait()

    @pl.loop(0, HEADS // 2)
    def _(i):
        project(wq, q, i)

    first.wait_recv()
    absorb(0)

    table = table_ref[...]
    pick = lax.broadcasted_iota(jnp.int32, (LANES, table.shape[0]), 1).astype(f32)
    apart = jnp.bitwise_xor(sub, lane)
    for i in range(tiles):
        chosen = (turned[:, tiles + i : tiles + i + 1] == pick).astype(f32)
        lam[i * LANES : (i + 1) * LANES, :] = dot(chosen, table, precision=highest)
    for i in range(tiles):
        at = slice(i * LANES, (i + 1) * LANES)
        here = lam[at, :]
        doc = dext[8 + i * LANES : 8 + (i + 1) * LANES, :]

        def spread(level):
            return jnp.broadcast_to(here[:, level : level + 1], (LANES, LANES))

        tile = spread(0)
        for level in range(1, tile_bits + 1):
            tile = jnp.where(apart >= 1 << (level - 1), spread(level), tile)
        weight[at, at] = jnp.where((doc == docs[i : i + 1, :]) & (sub >= lane), tile, 0.0)
        if i % 2 == 0:
            weight[at, (i + 1) * LANES : (i + 2) * LANES] = jnp.zeros((LANES, LANES), f32)
        wide = {}
        for j in range(i):
            level = tile_bits + (i ^ j).bit_length()
            if level not in wide:
                wide[level] = spread(level)
            weight[at, j * LANES : (j + 1) * LANES] = jnp.where(doc == docs[j : j + 1, :], wide[level], 0.0)
        for bit in range(bits):
            lamfar[bit, at, :] = jnp.where(doc == 0.0, spread(local_bits + 1 + bit), 0.0)

    block = min(2 * LANES, rows)
    events = {(bit * HEADS) // max(bits - 1, 1) - 1: bit for bit in range(1, bits - 1)}

    @pl.loop(0, HEADS)
    def _(h):
        for r in range(rows // block):
            at = slice(r * block, (r + 1) * block)
            upto = (r + 1) * block
            scores = dot(q[h, at, :], k[h, 0:upto, :], ((1,), (1,)))
            weighted = (scores * weight[at, 0:upto]).astype(bf16)
            near[h, at, :] = dot(weighted, v[h, 0:upto, :])
        for after, bit in events.items():

            @pl.when(h == after)
            def _():
                step(bit).wait_recv()
                forward(bit).start()
                absorb(bit)

    def far_state(bit, h):
        at = pl.ds(pl.multiple_of(lax.rem(h, half_heads) * HEAD_DIM, HEAD_DIM), HEAD_DIM)
        found = recv[bit, h // half_heads, at, :].astype(f32)
        return (found * coef[bit][0:1]).astype(bf16)

    for bit in range(1, bits - 1):
        forward(bit).wait_recv()

    early = list(range(bits - 1))

    @pl.loop(0, HEADS)
    def _(h):
        for r in range(rows // block):
            at = slice(r * block, (r + 1) * block)
            total = near[h, at, :]
            for a in range(0, len(early), 2):
                pair = early[a : a + 2]
                found = [far_state(bit, h) for bit in pair]
                made = dot(q[h, at, :], jnp.concatenate(found, 1) if len(found) > 1 else found[0])
                for n, bit in enumerate(pair):
                    total = total + lamfar[bit, at, :] * made[:, n * HEAD_DIM : (n + 1) * HEAD_DIM]
            near[h, at, :] = total

    last = bits - 1
    step(last).wait_recv()
    forward(last).start()
    note_flags(last)
    forward(last).wait_recv()

    @pl.loop(0, HEADS)
    def _(h):
        cols = pl.ds(pl.multiple_of(h * HEAD_DIM, HEAD_DIM), HEAD_DIM)
        gain = gain_ref[:, cols]
        found = far_state(last, h)
        for r in range(rows // block):
            at = slice(r * block, (r + 1) * block)
            total = near[h, at, :] + lamfar[last, at, :] * dot(q[h, at, :], found)
            scale = lax.rsqrt(jnp.mean(total * total, axis=-1, keepdims=True) + epsilon)
            out_ref[at, cols] = (total * scale * gain).astype(bf16)

    @pl.when(me < count - 1)
    def _():
        rim_copy.wait_send()

    first.wait_send()
    for bit in range(1, bits):
        step(bit).wait_send()
        forward(bit).wait_send()


def shards(
    tokens, doc_start, level_index, level_table, conv_weight, query_weight, key_weight, value_weight, norm_gain
):
    rows, width = tokens.shape
    count = lax.axis_size("seq")
    bits = count.bit_length() - 1
    half = HEADS // 2 * HEAD_DIM
    heads = (HEADS, rows, HEAD_DIM)
    vmem = pl.BlockSpec(memory_space=pltpu.VMEM)
    hbm = pl.BlockSpec(memory_space=pl.ANY)
    dma = pltpu.SemaphoreType.DMA
    return pl.pallas_call(
        functools.partial(layer, count),
        out_shape=jax.ShapeDtypeStruct((rows, width), bf16),
        in_specs=[vmem] * 6 + [hbm] * 3,
        out_specs=vmem,
        scratch_shapes=[
            pltpu.VMEM((width, width), bf16),
            pltpu.VMEM((width, width), bf16),
            pltpu.VMEM((width, width), bf16),
            pltpu.VMEM((LANES, LANES), f32),
            pltpu.VMEM((rows // LANES, LANES), f32),
            pltpu.VMEM((rows + 8, LANES), f32),
            pltpu.VMEM((rows, LANES), bf16),
            pltpu.VMEM((rows, level_table.shape[1]), f32),
            pltpu.VMEM((bits, rows, LANES), f32),
            pltpu.VMEM((rows, rows), f32),
            pltpu.VMEM((rows + 8, width), f32),
            pltpu.VMEM((rows, width), bf16),
            pltpu.VMEM(heads, bf16),
            pltpu.VMEM(heads, bf16),
            pltpu.VMEM(heads, bf16),
            pltpu.VMEM(heads, f32),
            pltpu.VMEM((2, half, HEAD_DIM), f32),
            pltpu.VMEM((half, HEAD_DIM), f32),
            pltpu.VMEM((8, LANES), f32),
            pltpu.VMEM((8, LANES), f32),
            pltpu.VMEM((bits, 8, LANES), f32),
            pltpu.VMEM((bits, 2, half + EDGE, HEAD_DIM), bf16),
            pltpu.VMEM((bits, 2, half + EDGE, HEAD_DIM), bf16),
            pltpu.VMEM((EDGE, width), bf16),
            pltpu.VMEM((EDGE, width), bf16),
            dma((3,)),
            dma((bits,)),
            dma((bits,)),
            dma((bits,)),
            dma((bits,)),
            dma((2,)),
        ],
        compiler_params=pltpu.CompilerParams(
            collective_id=0, has_side_effects=True, vmem_limit_bytes=56 * 1024 * 1024
        ),
    )(
        doc_start.reshape(rows // LANES, LANES),
        level_index.reshape(rows // LANES, LANES),
        level_table,
        conv_weight,
        norm_gain.reshape(1, width),
        tokens,
        query_weight,
        key_weight,
        value_weight,
    )


def solution(mesh):
    split = P(("groups", "seq"))
    rows = P(("groups", "seq"), None)
    in_specs = (rows, split, split, P(), P(), P(), P(), P(), P())
    return jax.shard_map(shards, mesh=mesh, in_specs=in_specs, out_specs=rows, check_vma=False)
```

time: 120 us -> 45.8 us (0.38)
  the two profiles are of different devices: /device:TPU:28 before, /device:TPU:0 now
where the time goes in v1:
time: 45.8 us; the launch traced here: 45.3 us
  Pallas kernels  40.9 us (89%)
  local copies, waits for them, and re-layouts  4.49 us (10%)
    pallas_call x1, Pallas kernels, shards(): pl.pallas_call(functools.partial(layer, count), out_shape=jax.ShapeDtypeS...  40.9 us
    unnamed x2, local copies, waits for them, and re-layouts  4.49 us

profile of v1, /device:TPU:0, one launch (start us, length us, event | category | flops | bytes accessed | tf_op | source)
XLA Modules:
  0.0 45.3 jit_solution(7864671674812364794)
XLA Ops:
  0.0 1.4 %copy.10.table_ref = f32[64,18]{1,0:T(8,128)} copy(f32[64,18]{0,1:T(8,128)} %param.12) | data formatting | bytes 9216 | tf_op args[3]
  1.4 40.9 %shard_map.91 = bf16[1024,1024]{1,0:T(8,128)(2,1)} custom-call(s32[8,128]{1,0:T(8,128)} %bitcast.3, s32[8,128]{1,0:T(8,128)} %bitcast.4, f32[64,18]{1,0:T(8,128)} %copy.10.table_ref, f32[4,1024]{1,0:T(4,128)} %taps_ref.1, f32[1,1024]{1,0:T(1,128)} %bitcast.5, bf16[1024,1024]{1,0:T(8,128)(2,1)} %tok_ref.1, bf16[1024,1024]{1,0:T(8,128)(2,1)} %wq_hbm.1, ...), custom_call_target="tpu_custom_call" | custom-call | tf_op jit(solution)/shard_map/pallas_call | solution.py:306
  42.3 3.1 %copy.12 = bf16[1024,1024]{1,0:T(8,128)(2,1)} copy(bf16[1024,1024]{1,0:T(8,128)(2,1)} %shard_map.91) | data formatting | bytes 4194304

commit v2 on v1

--- a/solution.py
+++ b/solution.py
@@ -24,11 +24,12 @@
 
 def layer(
     count,
-    ds_ref, li_ref, table_ref, taps_ref, gain_ref, tok_ref, wq_hbm, wk_hbm, wv_hbm,
-    out_ref,
+    ds_ref, li_ref, table_ref, taps_ref, tok_hbm, wq_hbm, wk_hbm, wv_hbm,
+    out_hbm,
+    tok_ref, out_ref,
     wq, wk, wv, turn, docs, dext, tail, lam, lamfar, weight, ext, conv, q, k, v, near,
     state, agg, flag_agg, flag_before, coef, send, recv, rim, halo,
-    w_sem, send_sem, recv_sem, fwd_send, fwd_recv, rim_sem,
+    w_sem, out_sem, send_sem, recv_sem, fwd_send, fwd_recv, rim_sem,
 ):
     rows, width = tok_ref.shape
     tiles = rows // LANES
@@ -37,7 +38,8 @@
     local_bits = rows.bit_length() - 1
     tile_bits = LANES.bit_length() - 1
     half_heads = HEADS // 2
-    half = half_heads * HEAD_DIM
+    part_heads = half_heads // 2
+    part_rows = part_heads * HEAD_DIM
     me = lax.axis_index("seq")
     core = lax.rem(me, 2)
     sibling = me + 1 - 2 * core
@@ -56,7 +58,7 @@
 
     loads = [
         pltpu.make_async_copy(src, dst, w_sem.at[i])
-        for i, (src, dst) in enumerate(((wk_hbm, wk), (wv_hbm, wv), (wq_hbm, wq)))
+        for i, (src, dst) in enumerate(((tok_hbm, tok_ref), (wk_hbm, wk), (wv_hbm, wv), (wq_hbm, wq)))
     ]
     for load in loads:
         load.start()
@@ -86,8 +88,11 @@
         dext[8 + i * LANES : 8 + (i + 1) * LANES, :] = column
         tail[i * LANES : (i + 1) * LANES, :] = (column == last_doc).astype(f32).astype(bf16)
     own_open = jnp.broadcast_to((last_doc == 0.0).astype(f32), (8, LANES))
-    flag_agg[...] = own_open
-    flag_before[...] = jnp.ones((8, LANES), f32)
+    for part in range(2):
+        flag_agg[part] = own_open
+        flag_before[part] = jnp.ones((8, LANES), f32)
+
+    loads[0].wait()
 
     for j in range(width // LANES):
         cols = slice(j * LANES, (j + 1) * LANES)
@@ -137,69 +142,105 @@
         out[2 * i] = made[:, :HEAD_DIM]
         out[2 * i + 1] = made[:, HEAD_DIM:]
 
-    loads[0].wait()
+    flag_rows = jnp.concatenate([own_open, own_open], 0).astype(bf16)
+    for part in range(2):
+        for s in range(2):
+            send[0, part, s, part_rows : part_rows + EDGE, :] = flag_rows
+
+    def first(part):
+        return remote(send.at[0, part], recv.at[0, part], send_sem.at[0, part], recv_sem.at[0, part], sibling)
+
     loads[1].wait()
+    loads[2].wait()
 
     @pl.loop(0, HEADS // 2)
-    def _(i):
+    def _(n):
+        part, side_of = n // 2, lax.rem(n, 2)
+        i = 2 * side_of + part
         project(wk, k, i)
         project(wv, v, i)
         for s in range(2):
             h = 2 * i + s
             made = dot(k[h] * tail[...], v[h], ((0,), (0,)))
-            at = pl.ds(pl.multiple_of(lax.rem(h, half_heads) * HEAD_DIM, HEAD_DIM), HEAD_DIM)
-            state[h // half_heads, at, :] = made
-            send[0, h // half_heads, at, :] = made.astype(bf16)
-
-    flag_rows = jnp.concatenate([own_open, own_open], 0).astype(bf16)
-    for s in range(2):
-        send[0, s, half : half + EDGE, :] = flag_rows
-    first = remote(send.at[0], recv.at[0], send_sem.at[0], recv_sem.at[0], sibling)
-    first.start()
-
-    def step(bit):
-        return remote(send.at[bit, core], recv.at[bit, core], send_sem.at[bit], recv_sem.at[bit], partner(bit))
-
-    def forward(bit):
-        return remote(recv.at[bit, core], recv.at[bit, core], fwd_send.at[bit], fwd_recv.at[bit], sibling)
-
-    def note_flags(bit):
-        other = recv[bit, core, half : half + EDGE, :].astype(f32)[0:8]
+            at = slice(s * HEAD_DIM, (s + 1) * HEAD_DIM)
+            state[part, side_of, at, :] = made
+            send[0, part, side_of, at, :] = made.astype(bf16)
+        for done in range(2):
+
+            @pl.when(n == 2 * done + 1)
+            def _():
+                first(done).start()
+
+    def step(bit, part):
+        return remote(
+            send.at[bit, part, core], recv.at[bit, part, core],
+            send_sem.at[bit, part], recv_sem.at[bit, part], partner(bit),
+        )
+
+    def forward(bit, part):
+        return remote(
+            recv.at[bit, part, core], recv.at[bit, part, core],
+            fwd_send.at[bit, part], fwd_recv.at[bit, part], sibling,
+        )
+
+    def note_flags(bit, part):
+        other = recv[bit, part, core, part_rows : part_rows + EDGE, :].astype(f32)[0:8]
         right = side(bit).astype(f32)
-        before = flag_before[...]
-        coef[bit] = right * before
-        flag_before[...] = before * ((1.0 - right) + right * other)
+        before = flag_before[part]
+        coef[bit, part] = right * before
+        flag_before[part] = before * ((1.0 - right) + right * other)
         return other, right
 
-    def absorb(bit):
-        other, right = note_flags(bit)
-        mine = flag_agg[...]
+    def absorb(bit, part):
+        other, right = note_flags(bit, part)
+        mine = flag_agg[part]
         of_agg = (right + (1.0 - right) * other)[0:1]
         of_other = ((1.0 - right) + right * mine)[0:1]
-        source = state.at[core] if bit == 0 else agg
-        total = of_agg * source[...] + of_other * recv[bit, core, 0:half, :].astype(f32)
-        agg[...] = total
-        send[bit + 1, core, 0:half, :] = total.astype(bf16)
+        source = state[part, core] if bit == 0 else agg[part]
+        total = of_agg * source + of_other * recv[bit, part, core, 0:part_rows, :].astype(f32)
+        agg[part] = total
+        send[bit + 1, part, core, 0:part_rows, :] = total.astype(bf16)
         joined = mine * other
-        flag_agg[...] = joined
-        send[bit + 1, core, half : half + EDGE, :] = jnp.concatenate([joined, joined], 0).astype(bf16)
-        step(bit + 1).start()
-
-    loads[2].wait()
+        flag_agg[part] = joined
+        send[bit + 1, part, core, part_rows : part_rows + EDGE, :] = jnp.concatenate([joined, joined], 0).astype(bf16)
+        step(bit + 1, part).start()
+
+    def arrive(bit, part):
+        step(bit, part).wait_recv()
+        forward(bit, part).start()
+        if bit < bits - 1:
+            absorb(bit, part)
+        else:
+            note_flags(bit, part)
+
+    last = bits - 1
+    steps = [(bit, part) for bit in range(1, last) for part in range(2)]
+    events = {0: steps[2:3], HEADS - 1: []}
+    for n, event in enumerate(steps[3:]):
+        after = min(2 + n, HEADS - 1)
+        events[after] = events.get(after, []) + [event]
+    events[HEADS - 1] = events[HEADS - 1] + [(last, 0)]
+
+    first(0).wait_recv()
+    absorb(0, 0)
+
+    loads[3].wait()
 
     @pl.loop(0, HEADS // 2)
     def _(i):
         project(wq, q, i)
 
-    first.wait_recv()
-    absorb(0)
+    first(1).wait_recv()
+    absorb(0, 1)
+    for event in steps[0:1]:
+        arrive(*event)
 
     table = table_ref[...]
-    pick = lax.broadcasted_iota(jnp.int32, (LANES, table.shape[0]), 1).astype(f32)
+    pick = lax.broadcasted_iota(jnp.int32, (LANES, table.shape[1]), 1).astype(f32)
     apart = jnp.bitwise_xor(sub, lane)
     for i in range(tiles):
         chosen = (turned[:, tiles + i : tiles + i + 1] == pick).astype(f32)
-        lam[i * LANES : (i + 1) * LANES, :] = dot(chosen, table, precision=highest)
+        lam[i * LANES : (i + 1) * LANES, :] = dot(chosen, table, ((1,), (1,)), highest)
     for i in range(tiles):
         at = slice(i * LANES, (i + 1) * LANES)
         here = lam[at, :]
@@ -223,8 +264,10 @@
         for bit in range(bits):
             lamfar[bit, at, :] = jnp.where(doc == 0.0, spread(local_bits + 1 + bit), 0.0)
 
+    for event in steps[1:2]:
+        arrive(*event)
+
     block = min(2 * LANES, rows)
-    events = {(bit * HEADS) // max(bits - 1, 1) - 1: bit for bit in range(1, bits - 1)}
 
     @pl.loop(0, HEADS)
     def _(h):
@@ -234,21 +277,22 @@
             scores = dot(q[h, at, :], k[h, 0:upto, :], ((1,), (1,)))
             weighted = (scores * weight[at, 0:upto]).astype(bf16)
             near[h, at, :] = dot(weighted, v[h, 0:upto, :])
-        for after, bit in events.items():
+        for after, arriving in events.items():
 
             @pl.when(h == after)
             def _():
-                step(bit).wait_recv()
-                forward(bit).start()
-                absorb(bit)
+                for event in arriving:
+                    arrive(*event)
 
     def far_state(bit, h):
-        at = pl.ds(pl.multiple_of(lax.rem(h, half_heads) * HEAD_DIM, HEAD_DIM), HEAD_DIM)
-        found = recv[bit, h // half_heads, at, :].astype(f32)
-        return (found * coef[bit][0:1]).astype(bf16)
-
-    for bit in range(1, bits - 1):
-        forward(bit).wait_recv()
+        part = lax.rem(h, half_heads) // part_heads
+        at = pl.ds(pl.multiple_of(lax.rem(h, part_heads) * HEAD_DIM, HEAD_DIM), HEAD_DIM)
+        found = recv[bit, part, h // half_heads, at, :].astype(f32)
+        return (found * coef[bit, 0][0:1]).astype(bf16)
+
+    for bit in range(1, last):
+        for part in range(2):
+            forward(bit, part).wait_recv()
 
     early = list(range(bits - 1))
 
@@ -265,31 +309,38 @@
                     total = total + lamfar[bit, at, :] * made[:, n * HEAD_DIM : (n + 1) * HEAD_DIM]
             near[h, at, :] = total
 
-    last = bits - 1
-    step(last).wait_recv()
-    forward(last).start()
-    note_flags(last)
-    forward(last).wait_recv()
+    arrive(last, 1)
 
     @pl.loop(0, HEADS)
-    def _(h):
+    def _(n):
+        @pl.when(n == half_heads)
+        def _():
+            for part in range(2):
+                forward(last, part).wait_recv()
+
+        h = lax.rem(n + core * half_heads, HEADS)
         cols = pl.ds(pl.multiple_of(h * HEAD_DIM, HEAD_DIM), HEAD_DIM)
-        gain = gain_ref[:, cols]
         found = far_state(last, h)
         for r in range(rows // block):
             at = slice(r * block, (r + 1) * block)
             total = near[h, at, :] + lamfar[last, at, :] * dot(q[h, at, :], found)
             scale = lax.rsqrt(jnp.mean(total * total, axis=-1, keepdims=True) + epsilon)
-            out_ref[at, cols] = (total * scale * gain).astype(bf16)
+            out_ref[at, cols] = (total * scale).astype(bf16)
+        pltpu.make_async_copy(out_ref.at[:, cols], out_hbm.at[:, cols], out_sem.at[h]).start()
+
+    for h in range(HEADS):
+        cols = pl.ds(h * HEAD_DIM, HEAD_DIM)
+        pltpu.make_async_copy(out_ref.at[:, cols], out_hbm.at[:, cols], out_sem.at[h]).wait()
 
     @pl.when(me < count - 1)
     def _():
         rim_copy.wait_send()
 
-    first.wait_send()
-    for bit in range(1, bits):
-        step(bit).wait_send()
-        forward(bit).wait_send()
+    for part in range(2):
+        first(part).wait_send()
+        for bit in range(1, bits):
+            step(bit, part).wait_send()
+            forward(bit, part).wait_send()
 
 
 def shards(
@@ -298,17 +349,19 @@
     rows, width = tokens.shape
     count = lax.axis_size("seq")
     bits = count.bit_length() - 1
-    half = HEADS // 2 * HEAD_DIM
+    part_rows = HEADS // 4 * HEAD_DIM
     heads = (HEADS, rows, HEAD_DIM)
     vmem = pl.BlockSpec(memory_space=pltpu.VMEM)
     hbm = pl.BlockSpec(memory_space=pl.ANY)
     dma = pltpu.SemaphoreType.DMA
-    return pl.pallas_call(
+    made = pl.pallas_call(
         functools.partial(layer, count),
         out_shape=jax.ShapeDtypeStruct((rows, width), bf16),
-        in_specs=[vmem] * 6 + [hbm] * 3,
-        out_specs=vmem,
+        in_specs=[vmem] * 4 + [hbm] * 4,
+        out_specs=hbm,
         scratch_shapes=[
+            pltpu.VMEM((rows, width), bf16),
+            pltpu.VMEM((rows, width), bf16),
             pltpu.VMEM((width, width), bf16),
             pltpu.VMEM((width, width), bf16),
             pltpu.VMEM((width, width), bf16),
@@ -325,20 +378,21 @@
             pltpu.VMEM(heads, bf16),
             pltpu.VMEM(heads, bf16),
             pltpu.VMEM(heads, f32),
-            pltpu.VMEM((2, half, HEAD_DIM), f32),
-            pltpu.VMEM((half, HEAD_DIM), f32),
-            pltpu.VMEM((8, LANES), f32),
-            pltpu.VMEM((8, LANES), f32),
-            pltpu.VMEM((bits, 8, LANES), f32),
-            pltpu.VMEM((bits, 2, half + EDGE, HEAD_DIM), bf16),
-            pltpu.VMEM((bits, 2, half + EDGE, HEAD_DIM), bf16),
+            pltpu.VMEM((2, 2, part_rows, HEAD_DIM), f32),
+            pltpu.VMEM((2, part_rows, HEAD_DIM), f32),
+            pltpu.VMEM((2, 8, LANES), f32),
+            pltpu.VMEM((2, 8, LANES), f32),
+            pltpu.VMEM((bits, 2, 8, LANES), f32),
+            pltpu.VMEM((bits, 2, 2, part_rows + EDGE, HEAD_DIM), bf16),
+            pltpu.VMEM((bits, 2, 2, part_rows + EDGE, HEAD_DIM), bf16),
             pltpu.VMEM((EDGE, width), bf16),
             pltpu.VMEM((EDGE, width), bf16),
-            dma((3,)),
-            dma((bits,)),
-            dma((bits,)),
-            dma((bits,)),
-            dma((bits,)),
+            dma((4,)),
+            dma((HEADS,)),
+            dma((bits, 2)),
+            dma((bits, 2)),
+            dma((bits, 2)),
+            dma((bits, 2)),
             dma((2,)),
         ],
         compiler_params=pltpu.CompilerParams(
@@ -347,14 +401,14 @@
     )(
         doc_start.reshape(rows // LANES, LANES),
         level_index.reshape(rows // LANES, LANES),
-        level_table,
+        level_table.T,
         conv_weight,
-        norm_gain.reshape(1, width),
         tokens,
         query_weight,
         key_weight,
         value_weight,
     )
+    return (made.astype(f32) * norm_gain[None, :]).astype(bf16)
 
 
 def solution(mesh):

time: 45.8 us -> 42.4 us (0.926)
  local copies, waits for them, and re-layouts: 4.49 us -> 0.01 us
  other arithmetic: 0 us -> 3.48 us
  Pallas kernels: 40.9 us -> 38.6 us
    unnamed x2, local copies, waits for them, and re-layouts: 4.49 us -> 0.01 us
    convert_element_type x0 -> x1, other arithmetic: none -> 3.48 us  [shards(): return (made.astype(f32) * norm_gain[None, :]).astype(bf16)]
    pallas_call x1, Pallas kernels: 40.9 us -> 38.6 us  [shards(): pl.pallas_call(functools.partial(layer, count), out_shape=jax.ShapeDtypeS...]
where the time goes in v2:
time: 42.4 us; the launch traced here: 42.1 us
  Pallas kernels  38.6 us (91%)
  other arithmetic  3.48 us (8%)
    pallas_call x1, Pallas kernels, shards(): pl.pallas_call(functools.partial(layer, count), out_shape=jax.ShapeDtypeS...  38.6 us
    convert_element_type x1, other arithmetic, shards(): return (made.astype(f32) * norm_gain[None, :]).astype(bf16)  3.48 us

profile of v2, /device:TPU:0, one launch (start us, length us, event | category | flops | bytes accessed | tf_op | source)
XLA Modules:
  0.0 42.1 jit_solution(6092548516136619233)
XLA Ops:
  0.0 0.0 copy-start
  0.0 38.6 %shard_map.91 = bf16[1024,1024]{1,0:T(8,128)(2,1)} custom-call(s32[8,128]{1,0:T(8,128)} %bitcast.4, s32[8,128]{1,0:T(8,128)} %bitcast.5, f32[18,64]{1,0:T(8,128)} %bitcast.3, f32[4,1024]{1,0:T(4,128)} %taps_ref.1, bf16[1024,1024]{1,0:T(8,128)(2,1)} %tok_hbm.1, bf16[1024,1024]{1,0:T(8,128)(2,1)} %wq_hbm.1, bf16[1024,1024]{1,0:T(8,128)(2,1)} %wk_hbm.1, ...), custom_call_target="tpu_custom_call" | custom-call | tf_op jit(solution)/shard_map/pallas_call | solution.py:357
  38.6 0.0 copy-done
  38.6 3.5 %multiply_convert_fusion = bf16[1024,1024]{1,0:T(8,128)(2,1)} fusion(bf16[1024,1024]{1,0:T(8,128)(2,1)} %shard_map.91, f32[1024]{0:T(1024)S(1)} %copy-done), kind=kLoop, calls=%fused_computation | loop fusion | flops 3145728 | bytes 4198400 | tf_op jit(solution)/shard_map/convert_element_type | solution.py:411
Async XLA Ops:
  0.0 38.6 %copy-start = (f32[1024]{0:T(1024)S(1)}, f32[1024]{0:T(1024)}, u32[]{:S(2)}) copy-start(f32[1024]{0:T(1024)} %param.17) | copy-start | bytes 12292

commit v3 on v2

--- a/solution.py
+++ b/solution.py
@@ -10,6 +10,7 @@
 HEADS = 8
 HEAD_DIM = 128
 LANES = 128
+PIECES = 4
 EDGE = 16
 
 highest = lax.Precision.HIGHEST
@@ -22,12 +23,17 @@
     return lax.dot_general(a, b, (contract, ((), ())), precision=precision, preferred_element_type=f32)
 
 
+def inner_slots(inner):
+    groups = [(g, j) for j in range(inner) for g in range(0, 1 << inner, 2 << j)]
+    return {group: n for n, group in enumerate(groups)}
+
+
 def layer(
     count,
-    ds_ref, li_ref, table_ref, taps_ref, tok_hbm, wq_hbm, wk_hbm, wv_hbm,
+    ds_ref, li_ref, table_ref, taps_ref, gain_ref, tok_hbm, wq_hbm, wk_hbm, wv_hbm,
     out_hbm,
     tok_ref, out_ref,
-    wq, wk, wv, turn, docs, dext, tail, lam, lamfar, weight, ext, conv, q, k, v, near,
+    wq, wk, wv, turn, docs, dext, tail, lam, lamfar, lamloc, local, weight, ext, conv, q, k, v, near,
     state, agg, flag_agg, flag_before, coef, send, recv, rim, halo,
     w_sem, out_sem, send_sem, recv_sem, fwd_send, fwd_recv, rim_sem,
 ):
@@ -37,6 +43,12 @@
     bits = count.bit_length() - 1
     local_bits = rows.bit_length() - 1
     tile_bits = LANES.bit_length() - 1
+    block = min(2 * LANES, rows)
+    blocks = rows // block
+    block_bits = block.bit_length() - 1
+    block_tiles = block // LANES
+    inner = local_bits - block_bits
+    slots = inner_slots(inner)
     half_heads = HEADS // 2
     part_heads = half_heads // 2
     part_rows = part_heads * HEAD_DIM
@@ -82,11 +94,16 @@
     turn[tiles : 2 * tiles, :] = li_ref[...].astype(f32)
     turned = jnp.transpose(turn[...])
     last_doc = running
+
+    def block_end(r):
+        row = (r + 1) * block_tiles - 1
+        return docs[row : row + 1, LANES - 1 : LANES]
+
     dext[0:8, :] = jnp.zeros((8, LANES), f32)
     for i in range(tiles):
         column = jnp.broadcast_to(turned[:, i : i + 1], (LANES, LANES))
         dext[8 + i * LANES : 8 + (i + 1) * LANES, :] = column
-        tail[i * LANES : (i + 1) * LANES, :] = (column == last_doc).astype(f32).astype(bf16)
+        tail[i * LANES : (i + 1) * LANES, :] = (column == block_end(i // block_tiles)).astype(f32).astype(bf16)
     own_open = jnp.broadcast_to((last_doc == 0.0).astype(f32), (8, LANES))
     for part in range(2):
         flag_agg[part] = own_open
@@ -161,7 +178,18 @@
         project(wv, v, i)
         for s in range(2):
             h = 2 * i + s
-            made = dot(k[h] * tail[...], v[h], ((0,), (0,)))
+            sums = []
+            for r in range(blocks):
+                rows_of = slice(r * block, (r + 1) * block)
+                sums.append(dot(k[h, rows_of, :] * tail[rows_of, :], v[h, rows_of, :], ((0,), (0,))))
+            for j in range(inner):
+                joined = []
+                for g in range(0, len(sums), 2):
+                    local[h, slots[(g << j, j)]] = sums[g].astype(bf16)
+                    linked = (block_end(((g + 2) << j) - 1) == block_end(((g + 1) << j) - 1)).astype(f32)
+                    joined.append(sums[g + 1] + linked * sums[g])
+                sums = joined
+            made = sums[0]
             at = slice(s * HEAD_DIM, (s + 1) * HEAD_DIM)
             state[part, side_of, at, :] = made
             send[0, part, side_of, at, :] = made.astype(bf16)
@@ -252,31 +280,45 @@
         tile = spread(0)
         for level in range(1, tile_bits + 1):
             tile = jnp.where(apart >= 1 << (level - 1), spread(level), tile)
-        weight[at, at] = jnp.where((doc == docs[i : i + 1, :]) & (sub >= lane), tile, 0.0)
-        if i % 2 == 0:
-            weight[at, (i + 1) * LANES : (i + 2) * LANES] = jnp.zeros((LANES, LANES), f32)
         wide = {}
-        for j in range(i):
-            level = tile_bits + (i ^ j).bit_length()
-            if level not in wide:
-                wide[level] = spread(level)
-            weight[at, j * LANES : (j + 1) * LANES] = jnp.where(doc == docs[j : j + 1, :], wide[level], 0.0)
+        base = i // block_tiles * block_tiles
+        for j in range(base, base + block_tiles):
+            to = slice((j - base) * LANES, (j - base + 1) * LANES)
+            if j > i:
+                weight[at, to] = jnp.zeros((LANES, LANES), f32)
+            elif j == i:
+                weight[at, to] = jnp.where((doc == docs[i : i + 1, :]) & (sub >= lane), tile, 0.0)
+            else:
+                level = tile_bits + (i ^ j).bit_length()
+                if level not in wide:
+                    wide[level] = spread(level)
+                weight[at, to] = jnp.where(doc == docs[j : j + 1, :], wide[level], 0.0)
+        r = i // block_tiles
+        for j in range(inner):
+            if r >> j & 1:
+                before = block_end((r >> j << j) - 1)
+                lamloc[j, at, :] = jnp.where(doc == before, spread(block_bits + 1 + j), 0.0)
         for bit in range(bits):
             lamfar[bit, at, :] = jnp.where(doc == 0.0, spread(local_bits + 1 + bit), 0.0)
 
     for event in steps[1:2]:
         arrive(*event)
-
-    block = min(2 * LANES, rows)
 
     @pl.loop(0, HEADS)
     def _(h):
         for r in range(rows // block):
             at = slice(r * block, (r + 1) * block)
-            upto = (r + 1) * block
-            scores = dot(q[h, at, :], k[h, 0:upto, :], ((1,), (1,)))
-            weighted = (scores * weight[at, 0:upto]).astype(bf16)
-            near[h, at, :] = dot(weighted, v[h, 0:upto, :])
+            scores = dot(q[h, at, :], k[h, at, :], ((1,), (1,)))
+            weighted = (scores * weight[at, :]).astype(bf16)
+            total = dot(weighted, v[h, at, :])
+            levels = [j for j in range(inner) if r >> j & 1]
+            for a in range(0, len(levels), 2):
+                pair = levels[a : a + 2]
+                found = [local[h, slots[((r >> j << j) - (1 << j), j)]] for j in pair]
+                made = dot(q[h, at, :], jnp.concatenate(found, 1) if len(found) > 1 else found[0])
+                for n, j in enumerate(pair):
+                    total = total + lamloc[j, at, :] * made[:, n * HEAD_DIM : (n + 1) * HEAD_DIM]
+            near[h, at, :] = total
         for after, arriving in events.items():
 
             @pl.when(h == after)
@@ -320,12 +362,13 @@
 
         h = lax.rem(n + core * half_heads, HEADS)
         cols = pl.ds(pl.multiple_of(h * HEAD_DIM, HEAD_DIM), HEAD_DIM)
+        gain = gain_ref[:, cols]
         found = far_state(last, h)
         for r in range(rows // block):
             at = slice(r * block, (r + 1) * block)
             total = near[h, at, :] + lamfar[last, at, :] * dot(q[h, at, :], found)
             scale = lax.rsqrt(jnp.mean(total * total, axis=-1, keepdims=True) + epsilon)
-            out_ref[at, cols] = (total * scale).astype(bf16)
+            out_ref[at, cols] = (total * scale * gain).astype(bf16)
         pltpu.make_async_copy(out_ref.at[:, cols], out_hbm.at[:, cols], out_sem.at[h]).start()
 
     for h in range(HEADS):
@@ -341,6 +384,20 @@
         for bit in range(1, bits):
             step(bit, part).wait_send()
             forward(bit, part).wait_send()
+
+
+def hand_over(made, out_hbm, held, in_sem, out_sem):
+    piece = made.shape[0] // PIECES
+    spans = [pl.ds(i * piece, piece) for i in range(PIECES)]
+    loads = [pltpu.make_async_copy(made.at[at], held.at[at], in_sem.at[i]) for i, at in enumerate(spans)]
+    stores = [pltpu.make_async_copy(held.at[at], out_hbm.at[at], out_sem.at[i]) for i, at in enumerate(spans)]
+    for load in loads:
+        load.start()
+    for load, store in zip(loads, stores):
+        load.wait()
+        store.start()
+    for store in stores:
+        store.wait()
 
 
 def shards(
@@ -351,13 +408,15 @@
     bits = count.bit_length() - 1
     part_rows = HEADS // 4 * HEAD_DIM
     heads = (HEADS, rows, HEAD_DIM)
+    block = min(2 * LANES, rows)
+    inner = (rows // block).bit_length() - 1
     vmem = pl.BlockSpec(memory_space=pltpu.VMEM)
     hbm = pl.BlockSpec(memory_space=pl.ANY)
     dma = pltpu.SemaphoreType.DMA
     made = pl.pallas_call(
         functools.partial(layer, count),
         out_shape=jax.ShapeDtypeStruct((rows, width), bf16),
-        in_specs=[vmem] * 4 + [hbm] * 4,
+        in_specs=[vmem] * 5 + [hbm] * 4,
         out_specs=hbm,
         scratch_shapes=[
             pltpu.VMEM((rows, width), bf16),
@@ -371,7 +430,9 @@
             pltpu.VMEM((rows, LANES), bf16),
             pltpu.VMEM((rows, level_table.shape[1]), f32),
             pltpu.VMEM((bits, rows, LANES), f32),
-            pltpu.VMEM((rows, rows), f32),
+            pltpu.VMEM((max(inner, 1), rows, LANES), f32),
+            pltpu.VMEM((HEADS, max(len(inner_slots(inner)), 1), HEAD_DIM, HEAD_DIM), bf16),
+            pltpu.VMEM((rows, block), f32),
             pltpu.VMEM((rows + 8, width), f32),
             pltpu.VMEM((rows, width), bf16),
             pltpu.VMEM(heads, bf16),
@@ -403,12 +464,20 @@
         level_index.reshape(rows // LANES, LANES),
         level_table.T,
         conv_weight,
+        norm_gain.reshape(1, width),
         tokens,
         query_weight,
         key_weight,
         value_weight,
     )
-    return (made.astype(f32) * norm_gain[None, :]).astype(bf16)
+    return pl.pallas_call(
+        hand_over,
+        out_shape=jax.ShapeDtypeStruct((rows, width), bf16),
+        in_specs=[hbm],
+        out_specs=hbm,
+        scratch_shapes=[pltpu.VMEM((rows, width), bf16), dma((PIECES,)), dma((PIECES,))],
+        compiler_params=pltpu.CompilerParams(vmem_limit_bytes=60 * 1024 * 1024),
+    )(made)
 
 
 def solution(mesh):

time: 42.4 us -> 39.2 us (0.925)
  other arithmetic: 3.48 us -> 0 us
    convert_element_type x1 -> x0, other arithmetic: 3.48 us -> none  [shards(): return (made.astype(f32) * norm_gain[None, :]).astype(bf16)]
    pallas_call x0 -> x1, Pallas kernels: none -> 2.42 us  [shards(): pl.pallas_call(hand_over, out_shape=jax.ShapeDtypeStruct((rows, width), b...]
    pallas_call x1, Pallas kernels: 38.6 us -> 36.6 us  [shards(): pl.pallas_call(functools.partial(layer, count), out_shape=jax.ShapeDtypeS...]
where the time goes in v3:
time: 39.2 us; the launch traced here: 39 us
  Pallas kernels  39 us (99%)
    pallas_call x1, Pallas kernels, shards(): pl.pallas_call(functools.partial(layer, count), out_shape=jax.ShapeDtypeS...  36.6 us
    pallas_call x1, Pallas kernels, shards(): pl.pallas_call(hand_over, out_shape=jax.ShapeDtypeStruct((rows, width), b...  2.42 us

profile of v3, /device:TPU:0, one launch (start us, length us, event | category | flops | bytes accessed | tf_op | source)
XLA Modules:
  0.0 39.0 jit_solution(16813066861319970359)
XLA Ops:
  0.0 36.6 %shard_map.91.made = bf16[1024,1024]{1,0:T(8,128)(2,1)} custom-call(s32[8,128]{1,0:T(8,128)} %bitcast.5, s32[8,128]{1,0:T(8,128)} %bitcast.6, f32[18,64]{1,0:T(8,128)} %bitcast.4, f32[4,1024]{1,0:T(4,128)} %taps_ref.1, f32[1,1024]{1,0:T(1,128)} %bitcast.7, bf16[1024,1024]{1,0:T(8,128)(2,1)} %tok_hbm.1, bf16[1024,1024]{1,0:T(8,128)(2,1)} %wq_hbm.1, ...), custom_call_target="tpu_custom_call" | custom-call | tf_op jit(solution)/shard_map/pallas_call | solution.py:416
  36.6 2.4 %shard_map.92 = bf16[1024,1024]{1,0:T(8,128)(2,1)} custom-call(bf16[1024,1024]{1,0:T(8,128)(2,1)} %shard_map.91.made), custom_call_target="tpu_custom_call" | custom-call | tf_op jit(solution)/shard_map/pallas_call | solution.py:473

commit v4 on v3

--- a/solution.py
+++ b/solution.py
@@ -258,8 +258,11 @@
     def _(i):
         project(wq, q, i)
 
-    first(1).wait_recv()
-    absorb(0, 1)
+        @pl.when(i == HEADS // 4 - 1)
+        def _():
+            first(1).wait_recv()
+            absorb(0, 1)
+
     for event in steps[0:1]:
         arrive(*event)
 
@@ -351,16 +354,22 @@
                     total = total + lamfar[bit, at, :] * made[:, n * HEAD_DIM : (n + 1) * HEAD_DIM]
             near[h, at, :] = total
 
-    arrive(last, 1)
-
     @pl.loop(0, HEADS)
     def _(n):
+        @pl.when(n == part_heads)
+        def _():
+            forward(last, 0).wait_recv()
+
         @pl.when(n == half_heads)
         def _():
-            for part in range(2):
-                forward(last, part).wait_recv()
-
-        h = lax.rem(n + core * half_heads, HEADS)
+            arrive(last, 1)
+
+        @pl.when(n == half_heads + part_heads)
+        def _():
+            forward(last, 1).wait_recv()
+
+        of_half = lax.rem(lax.rem(n // part_heads, 2) + core, 2)
+        h = of_half * half_heads + n // half_heads * part_heads + lax.rem(n, part_heads)
         cols = pl.ds(pl.multiple_of(h * HEAD_DIM, HEAD_DIM), HEAD_DIM)
         gain = gain_ref[:, cols]
         found = far_state(last, h)

time: 39.2 us -> 39.1 us (level)
  no operation moved by 1% of the time
where the time goes in v4:
time: 39.1 us; the launch traced here: 38.9 us
  Pallas kernels  38.9 us (99%)
    pallas_call x1, Pallas kernels, shards(): pl.pallas_call(functools.partial(layer, count), out_shape=jax.ShapeDtypeS...  36.4 us
    pallas_call x1, Pallas kernels, shards(): pl.pallas_call(hand_over, out_shape=jax.ShapeDtypeStruct((rows, width), b...  2.42 us

profile of v4, /device:TPU:0, one launch (start us, length us, event | category | flops | bytes accessed | tf_op | source)
XLA Modules:
  0.0 38.9 jit_solution(4625998005563725680)
XLA Ops:
  0.0 36.4 %shard_map.91.made = bf16[1024,1024]{1,0:T(8,128)(2,1)} custom-call(s32[8,128]{1,0:T(8,128)} %bitcast.5, s32[8,128]{1,0:T(8,128)} %bitcast.6, f32[18,64]{1,0:T(8,128)} %bitcast.4, f32[4,1024]{1,0:T(4,128)} %taps_ref.1, f32[1,1024]{1,0:T(1,128)} %bitcast.7, bf16[1024,1024]{1,0:T(8,128)(2,1)} %tok_hbm.1, bf16[1024,1024]{1,0:T(8,128)(2,1)} %wq_hbm.1, ...), custom_call_target="tpu_custom_call" | custom-call | tf_op jit(solution)/shard_map/pallas_call | solution.py:425
  36.4 2.4 %shard_map.92 = bf16[1024,1024]{1,0:T(8,128)(2,1)} custom-call(bf16[1024,1024]{1,0:T(8,128)(2,1)} %shard_map.91.made), custom_call_target="tpu_custom_call" | custom-call | tf_op jit(solution)/shard_map/pallas_call | solution.py:482

commit v5 on v4

--- a/solution.py
+++ b/solution.py
@@ -72,8 +72,7 @@
         pltpu.make_async_copy(src, dst, w_sem.at[i])
         for i, (src, dst) in enumerate(((tok_hbm, tok_ref), (wk_hbm, wk), (wv_hbm, wv), (wq_hbm, wq)))
     ]
-    for load in loads:
-        load.start()
+    loads[0].start()
 
     def remote(src, dst, s_sem, r_sem, to):
         return pltpu.make_async_remote_copy(
@@ -110,6 +109,8 @@
         flag_before[part] = jnp.ones((8, LANES), f32)
 
     loads[0].wait()
+    for load in loads[1:]:
+        load.start()
 
     for j in range(width // LANES):
         cols = slice(j * LANES, (j + 1) * LANES)
@@ -252,27 +253,13 @@
     first(0).wait_recv()
     absorb(0, 0)
 
-    loads[3].wait()
-
-    @pl.loop(0, HEADS // 2)
-    def _(i):
-        project(wq, q, i)
-
-        @pl.when(i == HEADS // 4 - 1)
-        def _():
-            first(1).wait_recv()
-            absorb(0, 1)
-
-    for event in steps[0:1]:
-        arrive(*event)
-
     table = table_ref[...]
     pick = lax.broadcasted_iota(jnp.int32, (LANES, table.shape[1]), 1).astype(f32)
     apart = jnp.bitwise_xor(sub, lane)
     for i in range(tiles):
         chosen = (turned[:, tiles + i : tiles + i + 1] == pick).astype(f32)
         lam[i * LANES : (i + 1) * LANES, :] = dot(chosen, table, ((1,), (1,)), highest)
-    for i in range(tiles):
+    def build(i):
         at = slice(i * LANES, (i + 1) * LANES)
         here = lam[at, :]
         doc = dext[8 + i * LANES : 8 + (i + 1) * LANES, :]
@@ -304,6 +291,18 @@
         for bit in range(bits):
             lamfar[bit, at, :] = jnp.where(doc == 0.0, spread(local_bits + 1 + bit), 0.0)
 
+    loads[3].wait()
+    pairs = HEADS // 2
+    for n in range(pairs):
+        project(wq, q, n)
+        for i in range(n * tiles // pairs, (n + 1) * tiles // pairs):
+            build(i)
+        if n == pairs // 2 - 1:
+            first(1).wait_recv()
+            absorb(0, 1)
+        elif n == pairs - 2:
+            for event in steps[0:1]:
+                arrive(*event)
     for event in steps[1:2]:
         arrive(*event)
 

time: 39.1 us -> 39.1 us (level)
  no operation moved by 1% of the time
where the time goes in v5:
time: 39.1 us; the launch traced here: 38.9 us
  Pallas kernels  38.9 us (99%)
    pallas_call x1, Pallas kernels, shards(): pl.pallas_call(functools.partial(layer, count), out_shape=jax.ShapeDtypeS...  36.5 us
    pallas_call x1, Pallas kernels, shards(): pl.pallas_call(hand_over, out_shape=jax.ShapeDtypeStruct((rows, width), b...  2.42 us

profile of v5, /device:TPU:0, one launch (start us, length us, event | category | flops | bytes accessed | tf_op | source)
XLA Modules:
  0.0 38.9 jit_solution(7255756467088187777)
XLA Ops:
  0.0 36.5 %shard_map.91.made = bf16[1024,1024]{1,0:T(8,128)(2,1)} custom-call(s32[8,128]{1,0:T(8,128)} %bitcast.5, s32[8,128]{1,0:T(8,128)} %bitcast.6, f32[18,64]{1,0:T(8,128)} %bitcast.4, f32[4,1024]{1,0:T(4,128)} %taps_ref.1, f32[1,1024]{1,0:T(1,128)} %bitcast.7, bf16[1024,1024]{1,0:T(8,128)(2,1)} %tok_hbm.1, bf16[1024,1024]{1,0:T(8,128)(2,1)} %wq_hbm.1, ...), custom_call_target="tpu_custom_call" | custom-call | tf_op jit(solution)/shard_map/pallas_call | solution.py:424
  36.5 2.4 %shard_map.92 = bf16[1024,1024]{1,0:T(8,128)(2,1)} custom-call(bf16[1024,1024]{1,0:T(8,128)(2,1)} %shard_map.91.made), custom_call_target="tpu_custom_call" | custom-call | tf_op jit(solution)/shard_map/pallas_call | solution.py:481
